TPU v7x, 128 devices: a whole 4x4x4 slice. The times are simulated.
128 devices in a mesh: replica: 16 (over y, z_hi, core), fsdp: 8 (over x, z_lo).
Axes of the slice: x: 4, y: 4, z: 4 (z_hi: 2, z_lo: 2; z = z_hi * 2 + z_lo), core: 2. Of those that a mesh axis runs over, the one named last changes fastest.
Arguments:
- tokens: bfloat16 [16, 3072, 8192], P('replica', 'fsdp'), may hold values from -6 to 6
- queries: bfloat16 [16, 3072, 4096], P('replica', 'fsdp'), may hold values from -250 to 250
- kv_weight: bfloat16 [16, 8192, 1024], P('replica', 'fsdp'), may hold values from -0.06629126 to 0.06629126
- doc_lengths: int32 [16, 8, 6], P('replica', 'fsdp'), may hold values from 1 to 192, 384 in all within a row
- local_params: bfloat16 [16, 1536, 8192], P('replica', 'fsdp'), may hold values from -6 to 6
- base_copy: bfloat16 [1536, 8192], P('fsdp'), may hold values from -6 to 6
- master: float32 [1536, 8192], P('fsdp', 'replica'), may hold values from -6 to 6
- momentum: float32 [1536, 8192], P('fsdp', 'replica'), may hold values from -2 to 2
Outputs:
- attended: bfloat16 [16, 3072, 4096], P('replica', 'fsdp')
- new_master: float32 [1536, 8192], P('fsdp', 'replica')
- new_momentum: float32 [1536, 8192], P('fsdp', 'replica')
- fresh_params: bfloat16 [1536, 8192], P('fsdp')
Inputs may be any that keep to these rules, and one draw needn't show every extreme that they name: `doc_lengths`: each device's 6 lengths sum to 384, and the longest is exactly 192.
All inputs are finite; a program needn't handle non-finite values.
Results may differ from a plain program's by a relative error of at most 0.012.
The roundings to bfloat16 on the way count: a program that leaves them out, or rounds other values in their place, can miss the bound.
Values may be sent and summed in bfloat16 or wider, within the bound.
A program may use at most 192 MiB of HBM per device.

v0:
```python
import jax
import jax.numpy as jnp
from jax import lax
from jax.sharding import Mesh
from jax.sharding import PartitionSpec as P

HEAD_SIZE = 128
BLK = 128
FSDP = ("fsdp_0", "fsdp_1")
MOMENTUM_COEF = 0.9
OUTER_RATE = 0.7
QUANT_RANGE = 448.0


def summed_rows(total, axes):
    for axis in axes:
        total = lax.psum_scatter(total, axis, scatter_dimension=0, tiled=True)
    return total


def doc_mask(lengths, tok_count):
    doc_ends = jnp.cumsum(lengths)
    places = jnp.arange(tok_count, dtype=jnp.int32)
    doc_index = jnp.sum((places[:, None] >= doc_ends[None, :-1]).astype(jnp.int32), axis=1)
    same_doc = doc_index[:, None] == doc_index[None, :]
    return jnp.logical_and(same_doc, places[None, :] <= places[:, None])


def attend(query_rows, packed, lengths):
    tok_count = query_rows.shape[0]
    head_count = query_rows.shape[1] // HEAD_SIZE
    groups = packed.shape[1] // (2 * HEAD_SIZE)
    key_heads = packed[:, : groups * HEAD_SIZE].reshape(tok_count, groups, HEAD_SIZE)
    value_heads = packed[:, groups * HEAD_SIZE :].reshape(tok_count, groups, HEAD_SIZE)
    grouped = query_rows.reshape(tok_count, groups, head_count // groups, HEAD_SIZE)
    scores = jnp.einsum(
        "tgjd,sgd->gjts", grouped, key_heads, preferred_element_type=jnp.float32
    ) * HEAD_SIZE ** (-0.5)
    allowed = doc_mask(lengths, tok_count)
    scores = jnp.where(allowed[None, None], scores, -1e30)
    highest = jnp.max(scores, axis=-1, keepdims=True)
    expo = jnp.exp(scores - highest)
    attn_weights = (expo / jnp.sum(expo, axis=-1, keepdims=True)).astype(jnp.bfloat16)
    mixed = jnp.einsum(
        "gjts,sgd->tgjd", attn_weights, value_heads, preferred_element_type=jnp.float32
    )
    return mixed.reshape(tok_count, head_count * HEAD_SIZE).astype(jnp.bfloat16)


def shards(tokens, queries, kv_weight, doc_lengths, local_params, base_copy, master, momentum):
    own_tokens = tokens[0]
    own_queries = queries[0]
    lengths = doc_lengths[0, 0]
    columns = lax.all_to_all(own_tokens, FSDP, split_axis=1, concat_axis=0, tiled=True)
    weight_shard = kv_weight[0]
    packed = summed_rows(jnp.dot(columns, weight_shard, preferred_element_type=jnp.float32), FSDP)
    attended = attend(own_queries, packed.astype(jnp.bfloat16), lengths)[None]
    replicas = lax.axis_size("replica")
    row_count = base_copy.shape[0]
    full_width = base_copy.shape[1]
    block_count = full_width // BLK
    pseudo_grad = base_copy.astype(jnp.float32) - local_params[0].astype(jnp.float32)
    blocked = pseudo_grad.reshape(row_count, block_count, BLK)
    scales = ((jnp.max(jnp.abs(blocked), axis=-1) + 1e-06) / QUANT_RANGE).astype(jnp.bfloat16)
    encoded = (blocked / scales.astype(jnp.float32)[..., None]).astype(jnp.bfloat16)
    decoded = (encoded.astype(jnp.float32) * scales.astype(jnp.float32)[..., None]).reshape(
        row_count, full_width
    )
    summed = lax.psum_scatter(
        decoded.astype(jnp.bfloat16), "replica", scatter_dimension=1, tiled=True
    ).astype(jnp.float32)
    averaged = summed * (1.0 / replicas)
    new_momentum = MOMENTUM_COEF * momentum + averaged
    new_master = master - OUTER_RATE * (averaged + MOMENTUM_COEF * new_momentum)
    fresh_params = lax.all_gather(new_master.astype(jnp.bfloat16), "replica", axis=1, tiled=True)
    return (attended, new_master, new_momentum, fresh_params)


def solution(mesh):
    finer = Mesh(mesh.devices.reshape(mesh.shape["replica"], 4, 2), ("replica", "fsdp_0", "fsdp_1"))
    placed = (
        P("replica", FSDP, None),
        P("replica", FSDP, None),
        P("replica", FSDP, None),
        P("replica", FSDP, None),
        P("replica", FSDP, None),
        P(FSDP, None),
        P(FSDP, "replica"),
        P(FSDP, "replica"),
    )
    return jax.shard_map(
        shards,
        mesh=finer,
        in_specs=placed,
        out_specs=(P("replica", FSDP, None), P(FSDP, "replica"), P(FSDP, "replica"), P(FSDP, None)),
        check_vma=False,
    )
```

profile of v0, /device:TPU:1, one launch (start us, length us, event | category | flops | bytes accessed | tf_op | source)
XLA Modules:
  0.0 413.3 jit_solution(16304995047222612006)
XLA Ops:
  7.2 0.0 copy-start
  7.2 8.8 %copy.29 = bf16[1,384,8192]{1,2,0:T(8,128)(2,1)} copy(bf16[1,384,8192]{2,1,0:T(8,128)(2,1)} %param.8) | data formatting | bytes 12582912 | tf_op args[0]
  16.0 6.2 %all-to-all-start = ((bf16[384,8,1024]{0,2,1:T(8,128)(2,1)}), bf16[384,8,1024]{0,2,1:T(8,128)(2,1)}, u32[]{:S(2)}, u32[]{:S(2)}) async-start(bf16[384,8,1024]{0,2,1:T(8,128)(2,1)} %bitcast.52), calls=%async_computation | async-start | bytes 12582912 | tf_op jit(solution)/shard_map/all_to_all | solution.py:54
  22.2 0.0 reduce-scatter.8.cloned.1.call-start
  22.2 4.0 abs_bitcast_fusion
  26.2 3.8 copy.43
  30.0 4.5 %reduce_max.19 = f32[192,64]{1,0:T(8,128)S(1)} reduce(f32[192,64,128]{2,1,0:T(8,128)} %bitcast.53, f32[]{:T(128)} %constant.5.clone.1), dimensions={2}, to_apply=%region_6.7 | reduce | flops 1560576 | bytes 6340612 | tf_op jit(solution)/shard_map/reduce_max | solution.py:64
  34.5 0.0 copy-start.2
  34.5 0.0 copy-start.3
  34.5 1.8 div.29
  36.3 0.1 copy-done.2
  36.4 1.0 copy-done.3
  37.3 6.5 %fusion.7 = bf16[192,8192]{1,0:T(8,128)(2,1)} fusion(bf16[192,8192]{1,0:T(8,128)(2,1)S(1)} %copy-done.2, f32[24,8,64,128]{3,2,1,0:T(8,128)S(1)} %bitcast.54, bf16[1,192,8192]{2,1,0:T(8,128)(2,1)S(1)} %copy-done.3), kind=kLoop, calls=%fused_computation.12 | loop fusion | flops 12582912 | bytes 15728640 | tf_op jit(solution)/shard_map/convert_element_type | solution.py:70
  43.8 0.0 reduce-scatter.8.cloned.1.call-update
  43.9 0.0 reduce-scatter.4.cloned.1.call-start
  43.9 65.3 %all-to-all-done = bf16[384,8,1024]{0,2,1:T(8,128)(2,1)} async-done(((bf16[384,8,1024]{0,2,1:T(8,128)(2,1)}), bf16[384,8,1024]{0,2,1:T(8,128)(2,1)}, u32[]{:S(2)}, u32[]{:S(2)}) %all-to-all-start) | async-done | bytes 6291488 | tf_op jit(solution)/shard_map/all_to_all | solution.py:54
  109.2 8.7 %copy.30 = bf16[8,384,1024]{2,1,0:T(8,128)(2,1)} copy(bf16[8,384,1024]{1,2,0:T(8,128)(2,1)} %bitcast.1) | data formatting | bytes 12582912 | tf_op jit(solution)/shard_map/all_to_all | solution.py:54
  117.9 0.0 copy-done
  117.9 12.5 %fusion.11 = f32[3072,1024]{1,0:T(8,128)} fusion(bf16[3072,1024]{1,0:T(8,128)(2,1)} %bitcast.56, bf16[1,1024,1024]{2,1,0:T(8,128)(2,1)S(1)} %copy-done), kind=kOutput, calls=%fused_computation.18 | convolution fusion | flops 6442450944 | bytes 20971520 | tf_op jit(solution)/shard_map/dot_general | solution.py:56
  130.4 0.0 copy-start.4
  130.4 0.0 copy-start.5
  130.4 0.0 reduce-scatter.4.cloned.1.call-update
  130.4 0.0 copy-start.6
  130.4 0.2 all-gather.2.cloned.1.call-start
  130.6 1.4 reduce-scatter.8.cloned.1.call-done
  132.1 0.0 copy-done.4
  132.1 0.0 copy-done.5
  132.1 2.0 fusion.18
  134.1 0.0 all-gather.2.cloned.1.call-update
  134.1 0.0 reduce-scatter.6.cloned.1.call-start
  134.2 114.8 %reduce-scatter.4.cloned.1.call-done = f32[768,1024]{1,0:T(8,128)} async-done(((f32[3072,1024]{1,0:T(8,128)}), f32[768,1024]{1,0:T(8,128)}) %reduce-scatter.4.cloned.1.call-update) | async-done | bytes 3145744 | tf_op jit(solution)/shard_map/reduce_scatter | solution.py:17
  249.0 0.0 reduce-scatter.6.cloned.1.call-update
  249.0 4.4 %copy.42 = bf16[48,8,32,128]{3,2,1,0:T(8,128)(2,1)} copy(bf16[48,8,32,128]{3,1,2,0:T(8,128)(2,1)} %bitcast.57) | data formatting | bytes 6291456
  253.4 0.0 copy-done.6
  253.4 0.2 reduce-window.4
  253.6 0.1 convert_reduce_fusion
  253.7 0.1 fusion.13
  253.8 52.4 %all-gather.2.cloned.1.call-done = bf16[192,8192]{1,0:T(8,128)(2,1)} async-done(((bf16[192,512]{1,0:T(8,128)(2,1)}), bf16[192,8192]{1,0:T(8,128)(2,1)}) %all-gather.2.cloned.1.call-update) | async-done | bytes 3145744 | tf_op jit(solution)/shard_map/all_gather | solution.py:75
  306.2 46.3 %reduce-scatter.6.cloned.1.call-done = f32[384,1024]{1,0:T(8,128)} async-done(((f32[768,1024]{1,0:T(8,128)}), f32[384,1024]{1,0:T(8,128)}) %reduce-scatter.6.cloned.1.call-update) | async-done | bytes 1572880 | tf_op jit(solution)/shard_map/reduce_scatter | solution.py:17
  352.5 1.5 convert_element_type.66
  354.0 0.1 fusion.19
  354.1 0.2 copy.39
  354.3 0.1 reshape.95
  354.4 11.2 %fusion.8 = f32[4,384,384,8]{2,1,3,0:T(8,128)} fusion(bf16[384,4,8,128]{3,2,1,0:T(8,128)(2,1)} %bitcast.55, bf16[384,4,128,1]{2,1,0,3:T(4,128)(2,1)S(1)} %bitcast.59), kind=kOutput, calls=%fused_computation.15 | convolution fusion | flops 1207959552 | bytes 22413312 | tf_op jit(solution)/shard_map/tgjd,sgd->gjts/dot_general | solution.py:36
  365.7 22.6 %fusion.20 = (f32[4,8,384]{2,1,0:T(8,128)S(1)}, f32[4,8,384,384]{2,3,1,0:T(8,128)}) fusion(f32[4,384,384,8]{2,1,3,0:T(8,128)} %fusion.8, pred[384,384]{0,1:T(8,128)(4,1)S(1)} %fusion.13), kind=kOutput, calls=%fused_computation.35 | output fusion | flops 28311936 | bytes 37945344 | tf_op jit(solution)/shard_map/sub | solution.py:42
  388.3 9.8 %fusion.10 = bf16[4,128,8,384]{3,1,2,0:T(8,128)(2,1)} fusion(bf16[384,4,128,1]{0,2,3,1:T(8,128)(2,1)S(1)} %bitcast.60, f32[4,8,384,384]{2,3,1,0:T(8,128)} %get-tuple-element.26, f32[4,8,384]{2,1,0:T(8,128)S(1)} %get-tuple-element.25), kind=kOutput, calls=%fused_computation.17 | convolution fusion | flops 1218969600 | bytes 22462464 | tf_op jit(solution)/shard_map/gjts,sgd->tgjd/dot_general | solution.py:44
  398.1 0.0 copy-start.1
  398.1 4.8 %copy.35 = bf16[1,384,4096]{2,1,0:T(8,128)(2,1)} copy(bf16[1,384,4096]{1,2,0:T(8,128)(2,1)} %bitcast.58) | data formatting | bytes 6291456
  402.9 3.9 copy.51
  406.8 0.0 copy-done.1
  (2 shorter events, 0.0 us)
Async XLA Ops:
  7.2 110.7 %copy-start = (bf16[1,1024,1024]{2,1,0:T(8,128)(2,1)S(1)}, bf16[1,1024,1024]{2,1,0:T(8,128)(2,1)}, u32[]{:S(2)}) copy-start(bf16[1,1024,1024]{2,1,0:T(8,128)(2,1)} %param.10) | copy-start | bytes 6291460
  16.0 93.2 %all-to-all-start = ((bf16[384,8,1024]{0,2,1:T(8,128)(2,1)}), bf16[384,8,1024]{0,2,1:T(8,128)(2,1)}, u32[]{:S(2)}, u32[]{:S(2)}) async-start(bf16[384,8,1024]{0,2,1:T(8,128)(2,1)} %bitcast.52), calls=%async_computation | async-start | bytes 12582912 | tf_op jit(solution)/shard_map/all_to_all | solution.py:54
  22.2 109.9 %reduce-scatter.8.cloned.1.call-start = ((), (), s32[]{:S(2)}) async-start(), calls=%async_computation.6 | async-start | bytes 3342336 | tf_op jit(solution)/shard_map/reduce_scatter | solution.py:69
  34.5 1.9 copy-start.2
  34.5 2.8 copy-start.3
  43.9 205.1 %reduce-scatter.4.cloned.1.call-start = ((), (), s32[]{:S(2)}) async-start(), calls=%async_computation.4 | async-start | bytes 15728640 | tf_op jit(solution)/shard_map/reduce_scatter | solution.py:17
  130.4 1.7 copy-start.4
  130.4 1.7 copy-start.5
  130.4 123.0 %copy-start.6 = (s32[1,1,6]{2,1,0:T(1,128)S(1)}, s32[1,1,6]{2,1,0:T(1,128)}, u32[]{:S(2)}) copy-start(s32[1,1,6]{2,1,0:T(1,128)} %param.11) | copy-start | bytes 76
  130.4 175.8 %all-gather.2.cloned.1.call-start = ((), (), s32[]{:S(2)}) async-start(), calls=%async_computation.7 | async-start | bytes 3342336 | tf_op jit(solution)/shard_map/all_gather | solution.py:75
  134.1 218.4 %reduce-scatter.6.cloned.1.call-start = ((), (), s32[]{:S(2)}) async-start(), calls=%async_computation.5 | async-start | bytes 4718592 | tf_op jit(solution)/shard_map/reduce_scatter | solution.py:17
  398.1 8.6 %copy-start.1 = (bf16[1,1024,1024]{2,1,0:T(8,128)(2,1)S(1)}, bf16[1,1024,1024]{2,1,0:T(8,128)(2,1)}, u32[]{:S(2)}) copy-start(bf16[1,1024,1024]{2,1,0:T(8,128)(2,1)} %param.10) | copy-start | bytes 6291460
Sparse Core Ops, SparseCore 0:
  44.0 88.0 reduce-scatter.7
  134.5 114.3 reduce-scatter.3
  251.8 54.3 all-gather.1
  308.4 44.0 reduce-scatter.5
where the time goes:
time: 414 us; the launch traced here: 413 us
  waiting for transfers between devices  280 us (68%)
  other arithmetic  41.5 us (10%)
  local copies, waits for them, and re-layouts  37.5 us (9%)
  matrix products  33.6 us (8%)
  between operations  13.9 us (3%)
  starting transfers between devices  6.55 us (2%)
    reduce_scatter x2, waiting for transfers between devices, summed_rows(): total = lax.psum_scatter(total, axis, scatter_dimension=0, tiled=True)  161 us
    all_to_all x1, waiting for transfers between devices, shards(): lax.all_to_all(own_tokens, FSDP, split_axis=1, concat_axis=0, tiled=True)  65.3 us
    all_gather x1, waiting for transfers between devices, shards(): lax.all_gather(new_master.astype(jnp.bfloat16), 'replica', axis=1, tiled=...  52.4 us
    unnamed x19, local copies, waits for them, and re-layouts  26.7 us
    sub x1, other arithmetic, attend(): expo = jnp.exp(scores - highest)  22.6 us
    dot_general x1, matrix products, shards(): jnp.dot(columns, weight_shard, preferred_element_type=jnp.float32)  12.5 us
    dot_general x1, matrix products, attend(): jnp.einsum('tgjd,sgd->gjts', grouped, key_heads, preferred_element_type=j...  11.2 us
    dot_general x1, matrix products, attend(): jnp.einsum('gjts,sgd->tgjd', attn_weights, value_heads, preferred_element...  9.84 us
  transfers between devices with their start and end apart: 5, of which 5 were waited for; matrix products, arithmetic and copies ran while one was open for 12% of the time, Pallas kernels for 0%

commit v1 on v0

--- a/solution.py
+++ b/solution.py
@@ -10,6 +10,13 @@
 MOMENTUM_COEF = 0.9
 OUTER_RATE = 0.7
 QUANT_RANGE = 448.0
+
+
+def swapped_in(array, mesh_axis, d):
+    size = lax.axis_size(mesh_axis)
+    shards = jnp.stack([array for _ in range(size)])
+    shards = lax.all_to_all(shards, mesh_axis, split_axis=0, concat_axis=0)
+    return jnp.concatenate(shards, axis=d)
 
 
 def summed_rows(total, axes):
@@ -72,7 +79,7 @@
     averaged = summed * (1.0 / replicas)
     new_momentum = MOMENTUM_COEF * momentum + averaged
     new_master = master - OUTER_RATE * (averaged + MOMENTUM_COEF * new_momentum)
-    fresh_params = lax.all_gather(new_master.astype(jnp.bfloat16), "replica", axis=1, tiled=True)
+    fresh_params = swapped_in(new_master.astype(jnp.bfloat16), "replica", 1)
     return (attended, new_master, new_momentum, fresh_params)
 
 

time: 414 us -> 449 us (1.085)
  blocking collectives: 0 us -> 77.6 us
  waiting for transfers between devices: 280 us -> 235 us
    all_to_all x0 -> x1, blocking collectives: none -> 77.6 us  [shards(): lax.all_to_all(own_tokens, FSDP, split_axis=1, concat_axis=0, tiled=True)]
    reduce_scatter x1, waiting for transfers between devices: 1.43 us -> 78.4 us  [shards(): lax.psum_scatter(decoded.astype(jnp.bfloat16), 'replica', scatter_dimensi...]
    all_gather x1 -> x0, waiting for transfers between devices: 52.4 us -> none  [shards(): lax.all_gather(new_master.astype(jnp.bfloat16), 'replica', axis=1, tiled=...]
    reduce_scatter x2, waiting for transfers between devices: 161 us -> 115 us  [summed_rows(): total = lax.psum_scatter(total, axis, scatter_dimension=0, tiled=True)]
    all_to_all x1, waiting for transfers between devices: 65.3 us -> 40.6 us  [swapped_in(): shards = lax.all_to_all(shards, mesh_axis, split_axis=0, concat_axis=0)]
    unnamed x19 -> x18, local copies, waits for them, and re-layouts: 26.7 us -> 23.6 us
  transfers between devices with their start and end apart: 5 -> 4, of which waited for: 5 -> 4; matrix products, arithmetic and copies ran while one was open for 12% -> 8% of each run, Pallas kernels for 0% -> 0%
where the time goes in v1:
time: 449 us; the launch traced here: 448 us
  waiting for transfers between devices  235 us (52%)
  blocking collectives  77.6 us (17%)
  other arithmetic  41.9 us (9%)
  local copies, waits for them, and re-layouts  40.3 us (9%)
  matrix products  33.6 us (7%)
  between operations  13.8 us (3%)
  starting transfers between devices  6.48 us (1%)
    reduce_scatter x2, waiting for transfers between devices, summed_rows(): total = lax.psum_scatter(total, axis, scatter_dimension=0, tiled=True)  115 us
    reduce_scatter x1, waiting for transfers between devices, shards(): lax.psum_scatter(decoded.astype(jnp.bfloat16), 'replica', scatter_dimensi...  78.4 us
    all_to_all x1, blocking collectives, shards(): lax.all_to_all(own_tokens, FSDP, split_axis=1, concat_axis=0, tiled=True)  77.6 us
    all_to_all x1, waiting for transfers between devices, swapped_in(): shards = lax.all_to_all(shards, mesh_axis, split_axis=0, concat_axis=0)  40.6 us
    unnamed x18, local copies, waits for them, and re-layouts  23.6 us
    sub x1, other arithmetic, attend(): expo = jnp.exp(scores - highest)  23.1 us
    dot_general x1, matrix products, shards(): jnp.dot(columns, weight_shard, preferred_element_type=jnp.float32)  12.4 us
    dot_general x1, matrix products, attend(): jnp.einsum('tgjd,sgd->gjts', grouped, key_heads, preferred_element_type=j...  11.2 us
  transfers between devices with their start and end apart: 4, of which 4 were waited for; matrix products, arithmetic and copies ran while one was open for 8% of the time, Pallas kernels for 0%

profile of v1, /device:TPU:1, one launch (start us, length us, event | category | flops | bytes accessed | tf_op | source)
XLA Modules:
  0.0 448.3 jit_solution(15789187238926468514)
XLA Ops:
  7.2 0.0 copy-start
  7.2 0.0 reduce-scatter.4.cloned.1.call-start
  7.2 8.8 %copy.44 = bf16[1,384,8192]{1,2,0:T(8,128)(2,1)} copy(bf16[1,384,8192]{2,1,0:T(8,128)(2,1)} %param.8) | data formatting | bytes 12582912 | tf_op args[0]
  16.0 77.6 %all_to_all.24 = bf16[384,8,1024]{0,2,1:T(8,128)(2,1)} all-to-all(bf16[384,8,1024]{0,2,1:T(8,128)(2,1)} %bitcast.57), channel_id=1, replica_groups=mesh['replica'=16,'fsdp_0'=4,'fsdp_1'=2] {'fsdp_0','fsdp_1'}, dimensions={1} | all-to-all | bytes 12582912 | tf_op jit(solution)/shard_map/all_to_all | solution.py:61
  93.6 8.7 %copy.45 = bf16[8,384,1024]{2,1,0:T(8,128)(2,1)} copy(bf16[8,384,1024]{1,2,0:T(8,128)(2,1)} %bitcast.56) | data formatting | bytes 12582912 | tf_op jit(solution)/shard_map/all_to_all | solution.py:61
  102.3 0.0 copy-done
  102.3 12.4 %fusion.11 = f32[3072,1024]{1,0:T(8,128)} fusion(bf16[3072,1024]{1,0:T(8,128)(2,1)} %bitcast.60, bf16[1,1024,1024]{2,1,0:T(8,128)(2,1)S(1)} %copy-done), kind=kOutput, calls=%fused_computation.18 | convolution fusion | flops 6442450944 | bytes 20971520 | tf_op jit(solution)/shard_map/dot_general | solution.py:63
  114.7 0.0 reduce-scatter.4.cloned.1.call-update
  114.7 0.0 reduce-scatter.8.cloned.1.call-start
  114.8 4.0 abs_bitcast_fusion
  118.7 3.8 copy.60
  122.5 4.5 reduce_max.19
  127.0 0.0 copy-start.2
  127.0 0.0 copy-start.3
  127.1 1.8 div.29
  128.8 0.1 copy-done.2
  129.0 0.9 copy-done.3
  129.9 6.5 %fusion.7 = bf16[192,8192]{1,0:T(8,128)(2,1)} fusion(bf16[192,8192]{1,0:T(8,128)(2,1)S(1)} %copy-done.2, f32[24,8,64,128]{3,2,1,0:T(8,128)S(1)} %bitcast.58, bf16[1,192,8192]{2,1,0:T(8,128)(2,1)S(1)} %copy-done.3), kind=kLoop, calls=%fused_computation.12 | loop fusion | flops 12582912 | bytes 15728640 | tf_op jit(solution)/shard_map/convert_element_type | solution.py:77
  136.4 0.0 copy-start.4
  136.4 0.0 copy-start.5
  136.4 0.0 reduce-scatter.8.cloned.1.call-update
  136.5 0.2 reduce-scatter.6.cloned.1.call-start
  136.7 94.7 %reduce-scatter.4.cloned.1.call-done = f32[768,1024]{1,0:T(8,128)} async-done(((f32[3072,1024]{1,0:T(8,128)}), f32[768,1024]{1,0:T(8,128)}) %reduce-scatter.4.cloned.1.call-update) | async-done | bytes 3145744 | tf_op jit(solution)/shard_map/reduce_scatter | solution.py:24
  231.4 0.0 reduce-scatter.6.cloned.1.call-update
  231.4 78.4 %reduce-scatter.8.cloned.1.call-done = bf16[192,512]{1,0:T(8,128)(2,1)} async-done(((bf16[192,8192]{1,0:T(8,128)(2,1)}), bf16[192,512]{1,0:T(8,128)(2,1)}) %reduce-scatter.8.cloned.1.call-update) | async-done | bytes 196624 | tf_op jit(solution)/shard_map/reduce_scatter | solution.py:76
  309.8 0.0 copy-done.4
  309.8 0.0 copy-done.5
  309.8 1.9 fusion.18
  311.8 2.0 stack.2
  313.7 0.0 copy-start.6
  313.7 6.2 %all-to-all-start.1 = ((bf16[16,192,512]{2,1,0:T(8,128)(2,1)}), bf16[16,192,512]{2,1,0:T(8,128)(2,1)}, u32[]{:S(2)}, u32[]{:S(2)}) async-start(bf16[16,192,512]{2,1,0:T(8,128)(2,1)} %stack.2), calls=%async_computation.4 | async-start | bytes 6291456 | tf_op jit(solution)/shard_map/all_to_all | solution.py:18
  319.9 5.2 %copy.59 = bf16[48,8,32,128]{3,2,1,0:T(8,128)(2,1)} copy(bf16[48,8,32,128]{3,1,2,0:T(8,128)(2,1)} %bitcast.61) | data formatting | bytes 6291456
  325.2 0.0 copy-done.6
  325.2 0.2 reduce-window.4
  325.4 0.1 convert_reduce_fusion
  325.4 0.1 fusion.13
  325.6 40.6 %all-to-all-done.1 = bf16[16,192,512]{2,1,0:T(8,128)(2,1)} async-done(((bf16[16,192,512]{2,1,0:T(8,128)(2,1)}), bf16[16,192,512]{2,1,0:T(8,128)(2,1)}, u32[]{:S(2)}, u32[]{:S(2)}) %all-to-all-start.1) | async-done | bytes 3145760 | tf_op jit(solution)/shard_map/all_to_all | solution.py:18
  366.2 3.9 copy.58
  370.1 20.8 %reduce-scatter.6.cloned.1.call-done = f32[384,1024]{1,0:T(8,128)} async-done(((f32[768,1024]{1,0:T(8,128)}), f32[384,1024]{1,0:T(8,128)}) %reduce-scatter.6.cloned.1.call-update) | async-done | bytes 1572880 | tf_op jit(solution)/shard_map/reduce_scatter | solution.py:24
  391.0 1.5 convert_element_type.66
  392.5 0.1 fusion.19
  392.5 0.2 copy.55
  392.8 0.1 reshape.103
  392.9 11.2 %fusion.8 = f32[4,384,384,8]{2,1,3,0:T(8,128)} fusion(bf16[384,4,8,128]{3,2,1,0:T(8,128)(2,1)} %bitcast.59, bf16[384,4,128,1]{2,1,0,3:T(4,128)(2,1)S(1)} %bitcast.64), kind=kOutput, calls=%fused_computation.15 | convolution fusion | flops 1207959552 | bytes 22413312 | tf_op jit(solution)/shard_map/tgjd,sgd->gjts/dot_general | solution.py:43
  404.1 23.1 %fusion.20 = (f32[4,8,384]{2,1,0:T(8,128)S(1)}, f32[4,8,384,384]{2,3,1,0:T(8,128)}) fusion(f32[4,384,384,8]{2,1,3,0:T(8,128)} %fusion.8, pred[384,384]{0,1:T(8,128)(4,1)S(1)} %fusion.13), kind=kOutput, calls=%fused_computation.35 | output fusion | flops 28311936 | bytes 37945344 | tf_op jit(solution)/shard_map/sub | solution.py:49
  427.1 0.0 copy-start.1
  427.2 10.0 %fusion.10 = bf16[4,128,8,384]{3,1,2,0:T(8,128)(2,1)} fusion(bf16[384,4,128,1]{0,2,3,1:T(8,128)(2,1)S(1)} %bitcast.65, f32[4,8,384,384]{2,3,1,0:T(8,128)} %get-tuple-element.34, f32[4,8,384]{2,1,0:T(8,128)S(1)} %get-tuple-element.33), kind=kOutput, calls=%fused_computation.17 | convolution fusion | flops 1218969600 | bytes 22462464 | tf_op jit(solution)/shard_map/gjts,sgd->tgjd/dot_general | solution.py:51
  437.2 4.6 %copy.51 = bf16[1,384,4096]{2,1,0:T(8,128)(2,1)} copy(bf16[1,384,4096]{1,2,0:T(8,128)(2,1)} %bitcast.63) | data formatting | bytes 6291456
  441.8 0.0 copy-done.1
  (2 shorter events, 0.0 us)
Async XLA Ops:
  7.2 95.2 %copy-start = (bf16[1,1024,1024]{2,1,0:T(8,128)(2,1)S(1)}, bf16[1,1024,1024]{2,1,0:T(8,128)(2,1)}, u32[]{:S(2)}) copy-start(bf16[1,1024,1024]{2,1,0:T(8,128)(2,1)} %param.10) | copy-start | bytes 6291460
  7.2 224.2 %reduce-scatter.4.cloned.1.call-start = ((), (), s32[]{:S(2)}) async-start(), calls=%async_computation.5 | async-start | bytes 15728640 | tf_op jit(solution)/shard_map/reduce_scatter | solution.py:24
  114.7 195.1 %reduce-scatter.8.cloned.1.call-start = ((), (), s32[]{:S(2)}) async-start(), calls=%async_computation.7 | async-start | bytes 3342336 | tf_op jit(solution)/shard_map/reduce_scatter | solution.py:76
  127.0 2.0 copy-start.2
  127.0 2.9 copy-start.3
  136.4 173.4 %copy-start.4 = (f32[192,512]{1,0:T(8,128)S(1)}, f32[192,512]{1,0:T(8,128)}, u32[]{:S(2)}) copy-start(f32[192,512]{1,0:T(8,128)} %param.14) | copy-start | bytes 1179652
  136.4 173.4 %copy-start.5 = (f32[192,512]{1,0:T(8,128)S(1)}, f32[192,512]{1,0:T(8,128)}, u32[]{:S(2)}) copy-start(f32[192,512]{1,0:T(8,128)} %param.15) | copy-start | bytes 1179652
  136.5 254.5 %reduce-scatter.6.cloned.1.call-start = ((), (), s32[]{:S(2)}) async-start(), calls=%async_computation.6 | async-start | bytes 4718592 | tf_op jit(solution)/shard_map/reduce_scatter | solution.py:24
  313.7 11.4 %copy-start.6 = (s32[1,1,6]{2,1,0:T(1,128)S(1)}, s32[1,1,6]{2,1,0:T(1,128)}, u32[]{:S(2)}) copy-start(s32[1,1,6]{2,1,0:T(1,128)} %param.11) | copy-start | bytes 76
  313.7 52.5 %all-to-all-start.1 = ((bf16[16,192,512]{2,1,0:T(8,128)(2,1)}), bf16[16,192,512]{2,1,0:T(8,128)(2,1)}, u32[]{:S(2)}, u32[]{:S(2)}) async-start(bf16[16,192,512]{2,1,0:T(8,128)(2,1)} %stack.2), calls=%async_computation.4 | async-start | bytes 6291456 | tf_op jit(solution)/shard_map/all_to_all | solution.py:18
  427.1 14.7 %copy-start.1 = (bf16[1,1024,1024]{2,1,0:T(8,128)(2,1)S(1)}, bf16[1,1024,1024]{2,1,0:T(8,128)(2,1)}, u32[]{:S(2)}) copy-start(bf16[1,1024,1024]{2,1,0:T(8,128)(2,1)} %param.10) | copy-start | bytes 6291460
Sparse Core Ops, SparseCore 0:
  114.8 116.4 reduce-scatter.3
  236.0 73.8 reduce-scatter.7
  312.2 78.7 reduce-scatter.5
